TPU v7x, 256 devices: a whole 4x4x8 slice. The times are simulated.
256 devices in a mesh: frame: 16 (over y_lo, z), row: 16 (over y_hi, x, core).
Axes of the slice: x: 4, y: 4 (y_hi: 2, y_lo: 2; y = y_hi * 2 + y_lo), z: 8, core: 2. Of those that a mesh axis runs over, the one named last changes fastest.
Arguments:
- clip_tokens: bfloat16 [64, 32, 40, 1152], P('frame', 'row'), may hold values from -6 to 6
- modulation: float32 [6, 1152], replicated, may hold values from -3 to 3
- w_sqkv: bfloat16 [1152, 3456], P(None, 'frame'), may hold values from -1.5 to 1.5
- w_sout: bfloat16 [1152, 1152], P(None, 'frame'), may hold values from -0.1875 to 0.1875
- w_tqkv: bfloat16 [1152, 3456], P(None, 'frame'), may hold values from -1.5 to 1.5
- w_tout: bfloat16 [1152, 1152], P(None, 'frame'), may hold values from -0.1875 to 0.1875
Outputs:
- block_out: bfloat16 [64, 32, 40, 1152], P('frame', 'row')
All inputs are finite; a program needn't handle non-finite values.
Results may differ from a plain program's by a relative error of at most 0.009.
Values may be sent and summed in bfloat16 or wider, within the bound.
No kernel may reach another device: no remote copies, remote signals or barrier semaphores. Data moves between devices by JAX's collectives and lax.ppermute only.
A program may use at most 128 MiB of HBM per device.

v0:
```python
import jax
import jax.numpy as jnp
from jax import lax
from jax.sharding import PartitionSpec as P

HEADS = 16
HEAD_DIM = 72


def layer_norm(inputs):
    average = jnp.mean(inputs, axis=-1, keepdims=True)
    centered = inputs - average
    variance = jnp.mean(centered * centered, axis=-1, keepdims=True)
    return centered * lax.rsqrt(variance + 1e-06)


def modulate(inputs, shift, scale):
    return (layer_norm(inputs) * (1.0 + scale) + shift).astype(jnp.bfloat16)


def frame_attention(qkv_block):
    queries = qkv_block[:, 0]
    key_rows = qkv_block[:, 1]
    values = qkv_block[:, 2]
    scores = jnp.einsum("qhd,khd->hqk", queries, key_rows, preferred_element_type=jnp.float32)
    scores = scores / jnp.sqrt(jnp.float32(HEAD_DIM))
    peak_score = jnp.max(scores, axis=-1, keepdims=True)
    exp_scores = jnp.exp(scores - peak_score)
    weights = (exp_scores / jnp.sum(exp_scores, axis=-1, keepdims=True)).astype(jnp.bfloat16)
    return jnp.einsum("hqk,khd->qhd", weights, values, preferred_element_type=jnp.float32).astype(
        jnp.bfloat16
    )


def spatial_core(qkv_blocks):
    return lax.map(frame_attention, qkv_blocks)


def temporal_core(qkv_blocks):
    queries = qkv_blocks[:, :, 0]
    key_rows = qkv_blocks[:, :, 1]
    values = qkv_blocks[:, :, 2]
    scores = jnp.einsum("fphd,gphd->phfg", queries, key_rows, preferred_element_type=jnp.float32)
    scores = scores / jnp.sqrt(jnp.float32(HEAD_DIM))
    peak_score = jnp.max(scores, axis=-1, keepdims=True)
    exp_scores = jnp.exp(scores - peak_score)
    weights = (exp_scores / jnp.sum(exp_scores, axis=-1, keepdims=True)).astype(jnp.bfloat16)
    return jnp.einsum(
        "phfg,gphd->fphd", weights, values, preferred_element_type=jnp.float32
    ).astype(jnp.bfloat16)


def on_device(clip_tokens, modulation, w_sqkv, w_sout, w_tqkv, w_tout):
    frames_here, rows_here, patches, features = clip_tokens.shape
    local_rows = rows_here * patches
    clip_float = clip_tokens.astype(jnp.float32).reshape(frames_here * local_rows, features)
    normed = modulate(clip_float, modulation[0], modulation[1])
    qkv_s = jnp.dot(
        normed,
        lax.all_gather(w_sqkv, "frame", axis=1, tiled=True),
        preferred_element_type=jnp.float32,
    )
    qkv_s = qkv_s.astype(jnp.bfloat16).reshape(frames_here, local_rows, 3, HEADS, HEAD_DIM)
    attended = spatial_core(lax.all_to_all(qkv_s, "row", split_axis=3, concat_axis=1, tiled=True))
    out_s = lax.all_to_all(attended, "row", split_axis=1, concat_axis=2, tiled=True)
    out_s = out_s.reshape(frames_here * local_rows, features)
    spatial_proj = jnp.dot(
        out_s,
        lax.all_gather(w_sout, "frame", axis=1, tiled=True),
        preferred_element_type=jnp.float32,
    )
    residual_mid = clip_float + modulation[2] * spatial_proj
    normed_t = modulate(residual_mid, modulation[3], modulation[4])
    qkv_t = jnp.dot(
        normed_t,
        lax.all_gather(w_tqkv, "frame", axis=1, tiled=True),
        preferred_element_type=jnp.float32,
    )
    qkv_t = qkv_t.astype(jnp.bfloat16).reshape(frames_here, local_rows, 3, HEADS, HEAD_DIM)
    attended = temporal_core(
        lax.all_to_all(qkv_t, "frame", split_axis=1, concat_axis=0, tiled=True)
    )
    out_t = lax.all_to_all(attended, "frame", split_axis=0, concat_axis=1, tiled=True)
    out_t = out_t.reshape(frames_here * local_rows, features)
    temporal_proj = jnp.dot(
        out_t,
        lax.all_gather(w_tout, "frame", axis=1, tiled=True),
        preferred_element_type=jnp.float32,
    )
    block_out = residual_mid + modulation[5] * temporal_proj
    return block_out.astype(jnp.bfloat16).reshape(frames_here, rows_here, patches, features)


def solution(mesh):
    in_specs = (
        P("frame", "row", None, None),
        P(),
        P(None, "frame"),
        P(None, "frame"),
        P(None, "frame"),
        P(None, "frame"),
    )
    out_specs = P("frame", "row", None, None)
    return jax.shard_map(
        on_device, mesh=mesh, in_specs=in_specs, out_specs=out_specs, check_vma=False
    )
```

profile of v0, /device:TPU:32, one launch (start us, length us, event | category | flops | bytes accessed | tf_op | source)
XLA Modules:
  0.0 505.0 jit_solution(770489204586520831)
XLA Ops:
  6.5 0.0 all-gather.5.cloned.1.call-start
  6.5 0.7 all-gather.5.cloned.1.call-update
  7.3 0.0 all-gather.7.cloned.1.call-start
  7.3 0.7 all-gather.7.cloned.1.call-update
  8.0 0.0 all-gather.9.cloned.1.call-start
  8.1 0.7 all-gather.9.cloned.1.call-update
  8.7 1.3 convert_reduce_fusion
  10.1 0.1 div.41
  10.1 1.5 multiply_reduce_fusion.2
  11.6 0.1 rsqrt.20
  11.7 0.0 copy-done.5
  11.7 0.7 slice_reduce_fusion.1
  12.4 94.1 %all-gather.5.cloned.1.call-done = bf16[1152,3456]{0,1:T(8,128)(2,1)} async-done(((bf16[1152,216]{0,1:T(8,128)(2,1)}), bf16[1152,3456]{0,1:T(8,128)(2,1)}) %all-gather.5.cloned.1.call-update) | async-done | bytes 7962640 | tf_op jit(solution)/shard_map/all_gather | solution.py:60
  106.4 0.0 copy-done
  106.4 8.5 %convolution_convert_fusion.1 = bf16[320,3456]{1,0:T(8,128)(2,1)S(1)} fusion(bf16[1152,3456]{0,1:T(8,128)(2,1)} %all-gather.5.cloned.1.call-done, f32[1152]{0:T(1024)S(1)} %get-tuple-element.36, f32[1152]{0:T(1024)S(1)} %get-tuple-element.37, f32[320]{0:T(512)S(1)} %rsqrt.20, f32[320]{0:T(512)S(1)} %div.41, bf16[320,1152]{1,0:T(8,128)(2,1)S(1)} %bitcast.88), kind=kOutput, calls=%fused_computation.14 | convolution fusion | flops 2551357440 | bytes 10923520 | tf_op jit(solution)/shard_map/dot_general | solution.py:58
  115.0 7.8 %reshape.99 = bf16[4,80,3,16,72]{4,3,2,1,0:T(8,128)(2,1)} reshape(bf16[320,3456]{1,0:T(8,128)(2,1)S(1)} %convolution_convert_fusion.1) | data formatting | bytes 4423680 | tf_op jit(solution)/shard_map/reshape | solution.py:63
  122.8 6.5 %copy.37 = bf16[4,80,3,16,72]{1,4,2,0,3:T(8,128)(2,1)} copy(bf16[4,80,3,16,72]{4,3,2,1,0:T(8,128)(2,1)} %reshape.99) | data formatting | bytes 4423680 | tf_op jit(solution)/shard_map/reshape | solution.py:63
  129.3 6.5 %all-to-all-start = ((bf16[4,80,3,16,72]{1,4,2,0,3:T(8,128)(2,1)}), bf16[4,80,3,16,72]{1,4,2,0,3:T(8,128)(2,1)S(1)}, u32[]{:S(2)}, u32[]{:S(2)}) async-start(bf16[4,80,3,16,72]{1,4,2,0,3:T(8,128)(2,1)} %copy.37), calls=%async_computation | async-start | bytes 7077888 | tf_op jit(solution)/shard_map/all_to_all | solution.py:64
  135.9 47.5 %all-to-all-done = bf16[4,80,3,16,72]{1,4,2,0,3:T(8,128)(2,1)S(1)} async-done(((bf16[4,80,3,16,72]{1,4,2,0,3:T(8,128)(2,1)}), bf16[4,80,3,16,72]{1,4,2,0,3:T(8,128)(2,1)S(1)}, u32[]{:S(2)}, u32[]{:S(2)}) %all-to-all-start) | async-done | bytes 2211872 | tf_op jit(solution)/shard_map/all_to_all | solution.py:64
  183.4 3.2 copy.38
  186.6 5.7 %all_to_all.51 = bf16[4,1280,3,1,72]{1,4,2,0,3:T(8,128)(2,1)S(1)} reshape(bf16[4,16,80,3,1,72]{2,1,5,3,0,4:T(8,128)(2,1)} %copy.38) | data formatting | bytes 4423680 | tf_op jit(solution)/shard_map/all_to_all | solution.py:64
  192.3 0.0 copy-done.4
  192.3 13.4 %while.10 = (s32[]{:T(128)}, bf16[4,1280,1,72]{1,3,2,0:T(8,128)(2,1)S(1)}, bf16[4,1280,3,1,72]{1,4,3,2,0:T(8,128)(2,1)S(1)}, s32[]{:T(128)}) while((s32[]{:T(128)}, bf16[4,1280,1,72]{1,3,2,0:T(8,128)(2,1)S(1)}, bf16[4,1280,3,1,72]{1,4,3,2,0:T(8,128)(2,1)S(1)}, s32[]{:T(128)}) %tuple.44), condition=%wide.region_5.6_spmd, body=%wide.region_2.5_spmd.sunk | while | flops 483417600 | bytes 21535804 | solution.py:36
  192.4 1.1 fusion.38
  193.5 1.0 fusion.39
  194.4 1.2 fusion.40
  195.7 1.1 fusion.38
  196.8 1.0 fusion.39
  197.8 1.2 fusion.40
  199.1 1.1 fusion.38
  200.1 1.0 fusion.39
  201.1 1.2 fusion.40
  202.4 1.1 fusion.38
  203.5 1.0 fusion.39
  204.4 1.2 fusion.40
  205.7 1.6 copy.40
  207.3 26.5 %all_to_all.66 = bf16[4,1280,1,72]{3,0,2,1:T(4,128)(2,1)S(1)} all-to-all(bf16[4,1280,1,72]{3,0,2,1:T(4,128)(2,1)S(1)} %copy.40), channel_id=1, replica_groups=mesh['frame'=16,'row'=16] {'row'}, dimensions={1} | all-to-all | bytes 1474560 | tf_op jit(solution)/shard_map/all_to_all | solution.py:65
  233.7 0.8 copy.53
  234.6 1.6 reshape.100
  236.2 0.0 all-gather.7.cloned.1.call-done
  236.3 0.0 copy-done.1
  236.3 0.0 copy-done.7
  236.3 3.2 fusion.26
  239.5 1.1 copy-done.2
  240.6 0.3 multiply_reduce_fusion.1
  240.9 56.0 %all-gather.9.cloned.1.call-done = bf16[1152,3456]{0,1:T(8,128)(2,1)} async-done(((bf16[1152,216]{0,1:T(8,128)(2,1)}), bf16[1152,3456]{0,1:T(8,128)(2,1)}) %all-gather.9.cloned.1.call-update) | async-done | bytes 7962640 | tf_op jit(solution)/shard_map/all_gather | solution.py:76
  296.9 7.0 %convolution_convert_fusion = bf16[320,3456]{1,0:T(8,128)(2,1)S(1)} fusion(bf16[1152,3456]{0,1:T(8,128)(2,1)} %all-gather.9.cloned.1.call-done, f32[320,1152]{1,0:T(8,128)} %copy-done.2, f32[1152]{0:T(1024)S(1)} %get-tuple-element.39, f32[1152]{0:T(1024)S(1)} %copy-done.6, f32[320]{0:T(512)S(1)} %add_rsqrt_fusion.1, f32[320]{0:T(512)S(1)} %broadcast_multiply_fusion.1), kind=kOutput, calls=%fused_computation.13 | convolution fusion | flops 2550988800 | bytes 11660800 | tf_op jit(solution)/shard_map/dot_general | solution.py:74
  303.8 7.8 %reshape.101 = bf16[4,80,3,16,72]{4,3,2,1,0:T(8,128)(2,1)} reshape(bf16[320,3456]{1,0:T(8,128)(2,1)S(1)} %convolution_convert_fusion) | data formatting | bytes 4423680 | tf_op jit(solution)/shard_map/reshape | solution.py:79
  311.7 5.2 %copy.43 = bf16[4,80,3,16,72]{4,3,2,0,1:T(8,128)(2,1)} copy(bf16[4,80,3,16,72]{4,3,2,1,0:T(8,128)(2,1)} %reshape.101) | data formatting | bytes 4423680 | tf_op jit(solution)/shard_map/reshape | solution.py:79
  316.9 17.9 %all-to-all-start.2 = ((bf16[4,80,3,16,72]{4,3,2,0,1:T(8,128)(2,1)}), bf16[4,80,3,16,72]{4,3,2,0,1:T(8,128)(2,1)}, u32[]{:S(2)}, u32[]{:S(2)}) async-start(bf16[4,80,3,16,72]{4,3,2,0,1:T(8,128)(2,1)} %copy.43), calls=%async_computation.2 | async-start | bytes 7864320 | tf_op jit(solution)/shard_map/all_to_all | solution.py:81
  334.8 0.0 all-gather.11.cloned.1.call-start
  334.9 0.5 all-gather.11.cloned.1.call-update
  335.4 108.0 %all-to-all-done.2 = bf16[4,80,3,16,72]{4,3,2,0,1:T(8,128)(2,1)} async-done(((bf16[4,80,3,16,72]{4,3,2,0,1:T(8,128)(2,1)}), bf16[4,80,3,16,72]{4,3,2,0,1:T(8,128)(2,1)}, u32[]{:S(2)}, u32[]{:S(2)}) %all-to-all-start.2) | async-done | bytes 2211872 | tf_op jit(solution)/shard_map/all_to_all | solution.py:81
  443.4 4.3 copy.44
  447.7 0.8 fusion.13
  448.6 3.9 fusion.27
  452.5 0.6 fusion.12
  453.1 0.8 copy.46
  454.0 38.7 %all_to_all.67 = bf16[64,5,16,72]{3,2,1,0:T(8,128)(2,1)S(1)} all-to-all(bf16[64,5,16,72]{3,2,1,0:T(8,128)(2,1)S(1)} %copy.46), channel_id=1, replica_groups=mesh['frame'=16,'row'=16] {'frame'}, dimensions={0} | all-to-all | bytes 1474560 | tf_op jit(solution)/shard_map/all_to_all | solution.py:83
  492.7 0.2 copy.54
  492.9 1.7 reshape.102
  494.6 0.0 all-gather.11.cloned.1.call-done
  494.6 0.0 copy-done.3
  494.6 3.9 fusion.8
  (18 shorter events, 0.2 us)
Async XLA Ops:
  6.5 99.9 %copy-start = (bf16[4,2,40,1152]{3,2,1,0:T(8,128)(2,1)S(1)}, bf16[4,2,40,1152]{3,2,1,0:T(8,128)(2,1)}, u32[]{:S(2)}) copy-start(bf16[4,2,40,1152]{3,2,1,0:T(8,128)(2,1)} %param.8) | copy-start | bytes 2211844
  6.5 5.1 %copy-start.5 = (f32[6,1152]{1,0:T(8,128)S(1)}, f32[6,1152]{1,0:T(8,128)}, u32[]{:S(2)}) copy-start(f32[6,1152]{1,0:T(8,128)} %param.9) | copy-start | bytes 82948
  6.5 99.9 %all-gather.5.cloned.1.call-start = ((), (), s32[]{:S(2)}) async-start(), calls=%async_computation.4 | async-start | bytes 8460288 | tf_op jit(solution)/shard_map/all_gather | solution.py:60
  7.3 229.0 %all-gather.7.cloned.1.call-start = ((), (), s32[]{:S(2)}) async-start(), calls=%async_computation.5 | async-start | bytes 2820096 | tf_op jit(solution)/shard_map/all_gather | solution.py:69
  8.0 288.9 %all-gather.9.cloned.1.call-start = ((), (), s32[]{:S(2)}) async-start(), calls=%async_computation.6 | async-start | bytes 8460288 | tf_op jit(solution)/shard_map/all_gather | solution.py:76
  129.3 54.0 %all-to-all-start = ((bf16[4,80,3,16,72]{1,4,2,0,3:T(8,128)(2,1)}), bf16[4,80,3,16,72]{1,4,2,0,3:T(8,128)(2,1)S(1)}, u32[]{:S(2)}, u32[]{:S(2)}) async-start(bf16[4,80,3,16,72]{1,4,2,0,3:T(8,128)(2,1)} %copy.37), calls=%async_computation | async-start | bytes 7077888 | tf_op jit(solution)/shard_map/all_to_all | solution.py:64
  186.6 5.7 %copy-start.4 = (bf16[4,1280,1,72]{1,3,2,0:T(8,128)(2,1)S(1)}, bf16[4,1280,1,72]{1,3,2,0:T(8,128)(2,1)}, u32[]{:S(2)}) copy-start(bf16[4,1280,1,72]{1,3,2,0:T(8,128)(2,1)} %custom-call) | copy-start | bytes 2211844
  233.7 2.5 copy-start.1
  233.7 2.5 copy-start.7
  236.3 60.6 %copy-start.6 = (f32[1152]{0:T(1024)S(1)}, f32[1152]{0:T(1024)}, u32[]{:S(2)}) copy-start(f32[1152]{0:T(1024)} %get-tuple-element.40) | copy-start | bytes 13828
  239.5 1.1 copy-start.2
  316.9 126.6 %all-to-all-start.2 = ((bf16[4,80,3,16,72]{4,3,2,0,1:T(8,128)(2,1)}), bf16[4,80,3,16,72]{4,3,2,0,1:T(8,128)(2,1)}, u32[]{:S(2)}, u32[]{:S(2)}) async-start(bf16[4,80,3,16,72]{4,3,2,0,1:T(8,128)(2,1)} %copy.43), calls=%async_computation.2 | async-start | bytes 7864320 | tf_op jit(solution)/shard_map/all_to_all | solution.py:81
  334.8 159.8 %all-gather.11.cloned.1.call-start = ((), (), s32[]{:S(2)}) async-start(), calls=%async_computation.7 | async-start | bytes 2820096 | tf_op jit(solution)/shard_map/all_gather | solution.py:87
  492.7 1.9 copy-start.3
Sparse Core Ops, SparseCore 0:
  9.2 97.2 all-gather.4
  108.2 84.0 all-gather.6
  194.1 102.7 all-gather.8
  337.1 119.8 all-gather.10
where the time goes:
time: 506 us; the launch traced here: 505 us
  waiting for transfers between devices  308 us (61%)
  blocking collectives  65.2 us (13%)
  local copies, waits for them, and re-layouts  48.9 us (10%)
  matrix products  33.2 us (7%)
  starting transfers between devices  24.6 us (5%)
  between operations  13.3 us (3%)
  other arithmetic  11.5 us (2%)
    all_to_all x1, waiting for transfers between devices, on_device(): lax.all_to_all(qkv_t, 'frame', split_axis=1, concat_axis=0, tiled=True)  108 us
    all_gather x1, waiting for transfers between devices, on_device(): lax.all_gather(w_sqkv, 'frame', axis=1, tiled=True)  94.1 us
    all_gather x1, waiting for transfers between devices, on_device(): lax.all_gather(w_tqkv, 'frame', axis=1, tiled=True)  56 us
    all_to_all x1, waiting for transfers between devices, on_device(): lax.all_to_all(qkv_s, 'row', split_axis=3, concat_axis=1, tiled=True)  47.5 us
    all_to_all x1, blocking collectives, on_device(): lax.all_to_all(attended, 'frame', split_axis=0, concat_axis=1, tiled=True)  38.7 us
    all_to_all x1, blocking collectives, on_device(): lax.all_to_all(attended, 'row', split_axis=1, concat_axis=2, tiled=True)  26.5 us
    all_to_all x1, starting transfers between devices, on_device(): lax.all_to_all(qkv_t, 'frame', split_axis=1, concat_axis=0, tiled=True)  17.9 us
    reshape x2, local copies, waits for them, and re-layouts, on_device(): qkv_s.astype(jnp.bfloat16)  14.3 us
  transfers between devices with their start and end apart: 6, of which 4 were waited for; matrix products, arithmetic and copies ran while one was open for 12% of the time, Pallas kernels for 0%

commit v1 on v0

v1 whole, which is shorter than its diff:
```python
import functools
import math

import jax
import jax.numpy as jnp
from jax import lax
from jax.experimental import pallas as pl
from jax.experimental.pallas import tpu as pltpu
from jax.sharding import PartitionSpec as P

HEADS = 16
HEAD_DIM = 72
D = 1152
GROUP = 4 * HEAD_DIM
PAD = 80
BF = jnp.bfloat16
F32 = jnp.float32
SCALE = math.log2(math.e) / math.sqrt(HEAD_DIM)
VMEM = pl.BlockSpec(memory_space=pltpu.VMEM)
ANY = pl.BlockSpec(memory_space=pl.ANY)
NT = (((1,), (1,)), ((), ()))


def params(mib):
    return pltpu.CompilerParams(vmem_limit_bytes=mib * 1024 * 1024)


def normalize(inputs, shift, scale):
    average = jnp.mean(inputs, axis=-1, keepdims=True)
    centered = inputs - average
    variance = jnp.mean(centered * centered, axis=-1, keepdims=True)
    return (centered * lax.rsqrt(variance + 1e-06) * (1.0 + scale) + shift).astype(BF)


def place():
    r = lax.axis_index("row")
    return r >> 3, (r >> 1) & 3, r & 1


def repack_kernel(w_ref, out_ref):
    _, x, _ = place()
    for g in range(4):

        @pl.when(x == g)
        def _(g=g):
            cols = []
            for part in range(3):
                for h in range(4):
                    p = 16 * part + 4 * g + h
                    cols.append(w_ref[p // 3, :, 72 * (p % 3) : 72 * (p % 3) + 72])
            out_ref[...] = jnp.concatenate(cols, axis=1)


def join_kernel(w_ref, out_ref):
    out_ref[...] = jnp.concatenate([w_ref[i] for i in range(16)], axis=0)


def gate_kernel(*refs):
    refs[-1][...] = jnp.zeros_like(refs[-1])


def spatial_kernel(a, b, c_, d_, w0, w1, o_ref, w_scr, q_scr, k_scr, v_scr):
    yh, x, c = place()
    for s, w in enumerate((w0, w1)):
        w_scr[pl.ds(pl.multiple_of(576 * (c ^ s), 64), 576), :] = w[...]
    lane = lax.broadcasted_iota(jnp.int32, (320, 128 - HEAD_DIM), 1)
    zeros = jnp.zeros((320, 128 - HEAD_DIM), BF)
    ones = jnp.where(lane == 0, 1.0, 0.0).astype(BF)
    for i, ref in enumerate((a, b, c_, d_)):
        rows = slice(320 * i, 320 * i + 320)
        qkv = jnp.dot(ref[...], w_scr[...], preferred_element_type=F32)
        for h in range(4):
            lo = 72 * h
            q = (qkv[:, lo : lo + 72] * SCALE).astype(BF)
            k = qkv[:, GROUP + lo : GROUP + lo + 72].astype(BF)
            v = qkv[:, 2 * GROUP + lo : 2 * GROUP + lo + 72].astype(BF)
            q_scr[h, rows, :] = jnp.concatenate([q, zeros], axis=1)
            k_scr[h, rows, :] = jnp.concatenate([k, zeros], axis=1)
            v_scr[h, rows, :] = jnp.concatenate([v, ones], axis=1)

    def step(i, carry):
        heads = []
        for h in range(4):
            q = q_scr[h, pl.ds(pl.multiple_of(320 * i, 64), 320), :]
            s = lax.dot_general(q, k_scr[h], NT, preferred_element_type=F32)
            m = jnp.max(s, axis=-1, keepdims=True)
            p = jnp.exp2(s - m).astype(BF)
            o = jnp.dot(p, v_scr[h], preferred_element_type=F32)
            heads.append((o[:, :72] / o[:, 72:73]).astype(BF))
        out = jnp.concatenate(heads, axis=1)
        for t in range(4):
            dest = (yh ^ (t & 1)) * 8 + ((x - i) & 3) * 2 + (c ^ (t >> 1))
            o_ref[dest] = out[80 * t : 80 * t + 80]
        return carry

    lax.fori_loop(0, 4, step, 0)


def spread(frame_major):
    if frame_major:
        row = lax.broadcasted_iota(jnp.int32, (512, 320), 0)
        col = lax.broadcasted_iota(jnp.int32, (512, 320), 1)
    else:
        row = lax.broadcasted_iota(jnp.int32, (320, 512), 1)
        col = lax.broadcasted_iota(jnp.int32, (320, 512), 0)
    f, t = row >> 5, row & 31
    j = (t * 13) >> 6
    want = 80 * j + 5 * f + (t - 5 * j)
    return jnp.where((t < 20) & (col == want), 1.0, 0.0).astype(BF)


def compact(narrow):
    if narrow:
        wide = lax.broadcasted_iota(jnp.int32, (320, 512), 1)
        thin = lax.broadcasted_iota(jnp.int32, (320, 512), 0)
    else:
        wide = lax.broadcasted_iota(jnp.int32, (512, 320), 0)
        thin = lax.broadcasted_iota(jnp.int32, (512, 320), 1)
    f, t = wide >> 5, wide & 31
    return jnp.where((t < 20) & (thin == 20 * f + t), 1.0, 0.0).astype(BF)


def unpack_chunks(ref, scr):
    zeros = jnp.zeros((12, D), BF)
    for f in range(16):
        scr[32 * f : 32 * f + 32, :] = jnp.concatenate([ref[f], zeros], axis=0)
    return scr[...]


def both_halves(x, mine_ref, other_ref):
    c = lax.axis_index("row") & 1
    mine = lax.dot_general(x, mine_ref[...], NT, preferred_element_type=F32)
    other = lax.dot_general(x, other_ref[...], NT, preferred_element_type=F32)
    return jnp.where(c == 0, mine, other), jnp.where(c == 0, other, mine)


def middle_kernel(o_ref, clip_ref, mod_ref, mine_ref, other_ref, mid_ref, out_ref):
    groups = [
        jnp.concatenate([o_ref[8 * (j >> 1) + 2 * g + (j & 1)] for j in range(4)], axis=0) for g in range(4)
    ]
    total = jnp.concatenate(both_halves(jnp.concatenate(groups, axis=1), mine_ref, other_ref), axis=1)
    mid = clip_ref[...].astype(F32) + mod_ref[2:3, :] * total
    mid_ref[...] = mid
    normed = normalize(mid, mod_ref[3:4, :], mod_ref[4:5, :])
    out = jnp.dot(spread(True), normed, preferred_element_type=F32).astype(BF)
    for f in range(16):
        out_ref[f] = out[32 * f : 32 * f + 20]


def temporal_kernel(x_ref, mine_ref, other_ref, o_ref, scr):
    x = jnp.dot(compact(True), unpack_chunks(x_ref, scr), preferred_element_type=F32).astype(BF)
    halves = both_halves(x, mine_ref, other_ref)

    def part(p):
        lo = PAD * (p % 24)
        return halves[p // 24][:, lo : lo + PAD]

    row = lax.broadcasted_iota(jnp.int32, (320, 320), 0)
    col = lax.broadcasted_iota(jnp.int32, (320, 320), 1)
    same = lax.rem(row, 5) == lax.rem(col, 5)
    heads = []
    for h in range(HEADS):
        q = (part(h) * SCALE).astype(BF)
        k = part(16 + h).astype(BF)
        v = part(32 + h).astype(BF)
        s = lax.dot_general(q, k, NT, preferred_element_type=F32)
        s = jnp.where(same, s, -1e30)
        m = jnp.max(s, axis=-1, keepdims=True)
        p = jnp.exp2(s - m)
        total = jnp.sum(p, axis=-1, keepdims=True)
        o = jnp.dot(p.astype(BF), v, preferred_element_type=F32) / total
        heads.append(o[:, :72].astype(BF))
    o = jnp.concatenate(heads, axis=1)
    out = jnp.dot(compact(False), o, preferred_element_type=F32).astype(BF)
    for f in range(16):
        o_ref[f] = out[32 * f : 32 * f + 20]


def final_kernel(o_ref, mid_ref, mod_ref, mine_ref, other_ref, out_ref, scr):
    o = jnp.dot(spread(False), unpack_chunks(o_ref, scr), preferred_element_type=F32).astype(BF)
    y = jnp.concatenate(both_halves(o, mine_ref, other_ref), axis=1)
    out_ref[...] = (mid_ref[...] + mod_ref[5:6, :] * y).astype(BF)


def shift_x(value, d):
    pairs = [(r, (r & 9) | ((((r >> 1) + d) & 3) << 1)) for r in range(16)]
    return lax.ppermute(value, "row", pairs)


def swap_core(value):
    return lax.ppermute(value, "row", [(r, r ^ 1) for r in range(16)])


def swap_yh(value):
    return lax.ppermute(value, "row", [(r, r ^ 8) for r in range(16)])


def take_half(value):
    y_lo = lax.axis_index("frame") >> 3
    pairs = [
        (16 * f + r, 16 * (f ^ 8) + r) for f in range(16) for r in range(16) if f >> 3 != r & 1
    ]
    pairs = [(src, dst) for dst, src in pairs]
    moved = lax.ppermute(value, ("frame", "row"), pairs)
    c = lax.axis_index("row") & 1
    return jnp.where(c == y_lo, value, moved)


def gather_half(value):
    rings = [list(range(8)), list(range(8, 16))]
    return lax.all_gather(value, "frame", axis=0, tiled=True, axis_index_groups=rings)


def call(kernel, outs, n_in, scratch=(), mib=40, any_in=(), us=2):
    return pl.pallas_call(
        kernel,
        out_shape=outs,
        in_specs=[ANY if i in any_in else VMEM for i in range(n_in)],
        out_specs=jax.tree.map(lambda _: VMEM, outs),
        scratch_shapes=list(scratch),
        compiler_params=params(mib),
        cost_estimate=pl.CostEstimate(flops=us * 10**9, bytes_accessed=us * 10**6, transcendentals=0),
    )


def sds(shape, dtype=BF):
    return jax.ShapeDtypeStruct(shape, dtype)


def on_device(clip_tokens, modulation, w_sqkv, w_sout, w_tqkv, w_tout):
    frames_here, rows_here, patches, features = clip_tokens.shape
    tokens = rows_here * patches
    yh, x, c = place()

    clip = clip_tokens.reshape(frames_here, tokens, features)
    normed = normalize(clip.astype(F32), modulation[0], modulation[1])
    first = lax.dynamic_slice(w_sqkv, (576 * c, 0), (576, 216))
    normed, first, w_sout, w_tout = lax.optimization_barrier((normed, first, w_sout, w_tout))

    own = lax.dynamic_slice_in_dim(normed, 2 * yh, 2, 0)
    theirs = swap_yh(lax.dynamic_slice_in_dim(normed, 2 * (1 - yh), 2, 0))
    outs = gather_half(take_half(jnp.concatenate([w_sout.T, w_tout.T], axis=0)))
    first = lax.all_to_all(first.reshape(16, 36, 216), "frame", 0, 0, tiled=True)
    first, w_tqkv = lax.optimization_barrier((first, w_tqkv))
    second = call(repack_kernel, sds((36, 3 * GROUP)), 1)(first)
    give = jnp.stack([own[1 - c], theirs[1 - c]])
    keep = jnp.stack([own[c], theirs[c]])
    g1 = jnp.concatenate([keep, swap_core(give)], axis=0).reshape(320, D)
    g = [g1] + [shift_x(g1, d) for d in (1, 2, 3)]
    gate = call(gate_kernel, sds((8, 128), F32), 4, any_in=(0, 1, 2, 3), us=2000)(*g)
    second = lax.all_to_all(jnp.broadcast_to(second[None], (16, 36, 3 * GROUP)), "frame", 0, 0, tiled=True)
    tq = jnp.pad(w_tqkv.T.reshape(3, 72, D), ((0, 0), (0, 8), (0, 0))).reshape(3 * PAD, D)
    *g, second, tq, _ = lax.optimization_barrier((*g, second, take_half(tq), gate))
    w_mine = call(join_kernel, sds((576, 3 * GROUP)), 1)(second)
    w_other = swap_core(w_mine)
    t_mine = gather_half(tq)

    o_s = call(
        spatial_kernel,
        sds((16, tokens, GROUP)),
        6,
        scratch=[
            pltpu.VMEM((D, 3 * GROUP), BF),
            pltpu.VMEM((4, 1280, 128), BF),
            pltpu.VMEM((4, 1280, 128), BF),
            pltpu.VMEM((4, 1280, 128), BF),
        ],
        us=15,
    )(*g, w_mine, w_other)
    o_s, outs = lax.optimization_barrier((o_s, outs))
    outs_other = swap_core(outs)
    outs = outs.reshape(8, 2, 72, D)
    outs_other = outs_other.reshape(8, 2, 72, D)
    out_s = [v[:, 0].reshape(576, D) for v in (outs, outs_other)]
    out_t = [v[:, 1].reshape(576, D) for v in (outs, outs_other)]
    o_s = lax.all_to_all(o_s, "row", 0, 0, tiled=True)

    mid, chunks = call(middle_kernel, (sds((320, D), F32), sds((16, 20, D))), 5, us=4)(
        o_s, clip.reshape(320, D), modulation, *out_s
    )
    chunks, t_mine = lax.optimization_barrier((chunks, t_mine))
    t_other = swap_core(t_mine)
    chunks = lax.all_to_all(chunks, "frame", 0, 0, tiled=True)
    o_t = call(temporal_kernel, sds((16, 20, D)), 3, scratch=[pltpu.VMEM((512, D), BF)], us=12)(
        chunks, t_mine, t_other
    )
    o_t = lax.all_to_all(o_t, "frame", 0, 0, tiled=True)
    out = call(final_kernel, sds((320, D)), 5, scratch=[pltpu.VMEM((512, D), BF)], us=4)(
        o_t, mid, modulation, *out_t
    )
    return out.reshape(frames_here, rows_here, patches, features)


def solution(mesh):
    in_specs = (
        P("frame", "row", None, None),
        P(),
        P(None, "frame"),
        P(None, "frame"),
        P(None, "frame"),
        P(None, "frame"),
    )
    out_specs = P("frame", "row", None, None)
    return jax.shard_map(
        on_device, mesh=mesh, in_specs=in_specs, out_specs=out_specs, check_vma=False
    )
```

time: 506 us -> 230 us (0.45)
  waiting for transfers between devices: 308 us -> 62 us
  Pallas kernels: 0 us -> 33.7 us
  matrix products: 33.2 us -> 0 us
  local copies, waits for them, and re-layouts: 48.9 us -> 18 us
  starting transfers between devices: 24.6 us -> 35.8 us
  blocking collectives: 65.2 us -> 59.6 us
  other arithmetic: 11.5 us -> 5.99 us
    all_gather x4 -> x2, waiting for transfers between devices: 150 us -> 5.27 us  [gather_half(): lax.all_gather(value, 'frame', axis=0, tiled=True, axis_index_groups=rings)]
    all_to_all x2 -> x3, waiting for transfers between devices: 156 us -> 18.2 us  [the longest x1 10.7 us: on_device(): o_s = lax.all_to_all(o_s, 'row', 0, 0, tiled=True)]
    ppermute x0 -> x10, waiting for transfers between devices: none -> 38.5 us  [the longest x3 25.1 us: shift_x(): return lax.ppermute(value, 'row', pairs)]
    pallas_call x0 -> x6, Pallas kernels: none -> 33.7 us  [the longest x1 17 us: on_device(): call(spatial_kernel, sds((16, tokens, GROUP)), 6, scratch=[pltpu.VMEM((D,...]
    dot_general x14 -> x0, matrix products: 33.2 us -> none  [the longest x1 8.54 us: on_device(): jnp.dot(normed, lax.all_gather(w_sqkv, 'frame', axis=1, tiled=True), pref...]
    reshape x6 -> x1, local copies, waits for them, and re-layouts: 30.7 us -> 0.8 us  [on_device(): first.reshape(16, 36, 216)]
    ppermute x0 -> x10, starting transfers between devices: none -> 14.9 us  [the longest x2 6.91 us: take_half(): moved = lax.ppermute(value, ('frame', 'row'), pairs)]
    all_to_all x5 -> x0, local copies, waits for them, and re-layouts: 14.3 us -> none  [the longest x2 8.94 us: on_device(): lax.all_to_all(qkv_s, 'row', split_axis=3, concat_axis=1, tiled=True)]
  transfers between devices with their start and end apart: 6 -> 15, of which waited for: 4 -> 8; matrix products, arithmetic and copies ran while one was open for 12% -> 5% of each run, Pallas kernels for 0% -> 9%
where the time goes in v1:
time: 230 us; the launch traced here: 229 us
  waiting for transfers between devices  62 us (27%)
  blocking collectives  59.6 us (26%)
  starting transfers between devices  35.8 us (16%)
  Pallas kernels  33.7 us (15%)
  local copies, waits for them, and re-layouts  18 us (8%)
  between operations  13.7 us (6%)
  other arithmetic  5.99 us (3%)
    all_to_all x1, blocking collectives, on_device(): chunks = lax.all_to_all(chunks, 'frame', 0, 0, tiled=True)  31.5 us
    all_to_all x1, blocking collectives, on_device(): o_t = lax.all_to_all(o_t, 'frame', 0, 0, tiled=True)  28.1 us
    ppermute x3, waiting for transfers between devices, shift_x(): return lax.ppermute(value, 'row', pairs)  25.1 us
    pallas_call x1, Pallas kernels, on_device(): call(spatial_kernel, sds((16, tokens, GROUP)), 6, scratch=[pltpu.VMEM((D,...  17 us
    pallas_call x1, Pallas kernels, on_device(): call(temporal_kernel, sds((16, 20, D)), 3, scratch=[pltpu.VMEM((512, D),...  10.9 us
    ppermute x2, waiting for transfers between devices, take_half(): moved = lax.ppermute(value, ('frame', 'row'), pairs)  10.7 us
    all_to_all x1, waiting for transfers between devices, on_device(): o_s = lax.all_to_all(o_s, 'row', 0, 0, tiled=True)  10.7 us
    all_to_all x1, starting transfers between devices, on_device(): lax.all_to_all(first.reshape(16, 36, 216), 'frame', 0, 0, tiled=True)  10.5 us
  transfers between devices with their start and end apart: 15, of which 8 were waited for; matrix products, arithmetic and copies ran while one was open for 5% of the time, Pallas kernels for 9%

profile of v1, /device:TPU:32, one launch (start us, length us, event | category | flops | bytes accessed | tf_op | source)
XLA Modules:
  0.0 228.7 jit_solution(10201076499201115689)
XLA Ops:
  6.5 1.4 convert_reduce_fusion
  7.9 0.0 copy-start.11
  7.9 0.0 copy-start.12
  8.0 0.1 div.9
  8.1 1.5 multiply_reduce_fusion
  9.5 0.1 rsqrt.12
  9.6 0.9 add_reduce_fusion
  10.5 0.2 constant_dynamic-slice_fusion.5
  10.7 0.3 fusion.3
  11.1 3.5 %collective-permute-start.7 = (bf16[144,1152]{1,0:T(8,128)(2,1)S(1)}, bf16[144,1152]{1,0:T(8,128)(2,1)S(1)}, u32[]{:S(2)}, u32[]{:S(2)}) collective-permute-start(bf16[144,1152]{1,0:T(8,128)(2,1)S(1)} %pad_maximum_fusion.2), channel_id=1, source_target_pairs={{129,1},{131,3},{133,5},{135,7},{137,9},{139,11},{141,13},{143,15}... | collective-permute-start | bytes 995336 | tf_op jit(solution)/shard_map/ppermute | solution.py:204
  14.6 4.6 %collective-permute-done.7 = bf16[144,1152]{1,0:T(8,128)(2,1)S(1)} collective-permute-done((bf16[144,1152]{1,0:T(8,128)(2,1)S(1)}, bf16[144,1152]{1,0:T(8,128)(2,1)S(1)}, u32[]{:S(2)}, u32[]{:S(2)}) %collective-permute-start.7) | collective-permute-done | bytes 331808 | tf_op jit(solution)/shard_map/ppermute | solution.py:204
  19.2 0.8 broadcast_select_fusion.1
  20.0 0.0 all-gather.3.cloned.1.call-update
  20.0 0.2 copy.12
  20.2 0.8 reshape.63
  21.0 10.5 %all-to-all-start = ((bf16[16,36,216]{2,1,0:T(8,128)(2,1)}), bf16[16,36,216]{2,1,0:T(8,128)(2,1)S(1)}, u32[]{:S(2)}, u32[]{:S(2)}) async-start(bf16[16,36,216]{2,1,0:T(8,128)(2,1)} %reshape.63), calls=%async_computation | async-start | bytes 655360 | tf_op jit(solution)/shard_map/all_to_all | solution.py:243
  31.5 3.0 %collective-permute-start = (bf16[2,80,1152]{2,1,0:T(8,128)(2,1)S(1)}, bf16[2,80,1152]{2,1,0:T(8,128)(2,1)}, u32[]{:S(2)}, u32[]{:S(2)}) collective-permute-start(bf16[2,80,1152]{2,1,0:T(8,128)(2,1)S(1)} %constant_dynamic-slice_fusion.3), channel_id=1, source_target_pairs={{0,8},{1,9},{2,10},{3,11},{4,12},{5,13},{6,14},{7,15},{8,0},{9,1},... | collective-permute-start | bytes 1105928 | tf_op jit(solution)/shard_map/ppermute | solution.py:195
  34.5 7.5 %all-to-all-done.w_ref = bf16[16,36,216]{2,1,0:T(8,128)(2,1)S(1)} async-done(((bf16[16,36,216]{2,1,0:T(8,128)(2,1)}), bf16[16,36,216]{2,1,0:T(8,128)(2,1)S(1)}, u32[]{:S(2)}, u32[]{:S(2)}) %all-to-all-start) | async-done | bytes 248864 | tf_op jit(solution)/shard_map/all_to_all | solution.py:243
  42.0 0.1 shard_map.64
  42.1 1.1 broadcast_in_dim.2
  43.2 5.0 %all-to-all-start.1 = ((bf16[16,36,864]{2,1,0:T(8,128)(2,1)}), bf16[16,36,864]{2,1,0:T(8,128)(2,1)S(1)}, u32[]{:S(2)}, u32[]{:S(2)}) async-start(bf16[16,36,864]{2,1,0:T(8,128)(2,1)} %broadcast_in_dim.2), calls=%async_computation.1 | async-start | bytes 2293760 | tf_op jit(solution)/shard_map/all_to_all | solution.py:251
  48.3 0.0 all-gather.5.cloned.1.call-start
  48.3 0.0 copy-start.13
  48.4 0.0 collective-permute-done
  48.4 1.1 constant_dynamic-slice_fusion.2
  49.6 0.1 collective-permute-start.1
  49.7 3.4 %collective-permute-start.5 = (bf16[240,1152]{1,0:T(8,128)(2,1)S(1)}, bf16[240,1152]{1,0:T(8,128)(2,1)S(1)}, u32[]{:S(2)}, u32[]{:S(2)}) collective-permute-start(bf16[240,1152]{1,0:T(8,128)(2,1)S(1)} %bitcast.44), channel_id=1, source_target_pairs={{129,1},{131,3},{133,5},{135,7},{137,9},{139,11},{141,13},{143,15}... | collective-permute-start | bytes 1658888 | tf_op jit(solution)/shard_map/ppermute | solution.py:204
  53.1 0.0 collective-permute-done.1
  53.1 0.1 pad_maximum_fusion
  53.2 2.8 %collective-permute-start.4 = (bf16[320,1152]{1,0:T(8,128)(2,1)S(1)}, bf16[320,1152]{1,0:T(8,128)(2,1)}, u32[]{:S(2)}, u32[]{:S(2)}) collective-permute-start(bf16[320,1152]{1,0:T(8,128)(2,1)S(1)} %bitcast.39), channel_id=1, source_target_pairs={{0,6},{1,7},{2,0},{3,1},{4,2},{5,3},{6,4},{7,5},{8,14},{9,15},{10,... | collective-permute-start | bytes 2211848 | tf_op jit(solution)/shard_map/ppermute | solution.py:187
  56.1 0.8 collective-permute-start.3
  56.9 0.9 collective-permute-start.2
  57.8 6.2 %collective-permute-done.5 = bf16[240,1152]{1,0:T(8,128)(2,1)S(1)} collective-permute-done((bf16[240,1152]{1,0:T(8,128)(2,1)S(1)}, bf16[240,1152]{1,0:T(8,128)(2,1)S(1)}, u32[]{:S(2)}, u32[]{:S(2)}) %collective-permute-start.5) | collective-permute-done | bytes 552992 | tf_op jit(solution)/shard_map/ppermute | solution.py:204
  63.9 0.9 broadcast_select_fusion
  64.9 21.3 %collective-permute-done.4.d_ = bf16[320,1152]{1,0:T(8,128)(2,1)} collective-permute-done((bf16[320,1152]{1,0:T(8,128)(2,1)S(1)}, bf16[320,1152]{1,0:T(8,128)(2,1)}, u32[]{:S(2)}, u32[]{:S(2)}) %collective-permute-start.4) | collective-permute-done | bytes 737312 | tf_op jit(solution)/shard_map/ppermute | solution.py:187
  86.2 0.0 collective-permute-done.3.c_
  86.2 3.8 %collective-permute-done.2.b = bf16[320,1152]{1,0:T(8,128)(2,1)} collective-permute-done((bf16[320,1152]{1,0:T(8,128)(2,1)S(1)}, bf16[320,1152]{1,0:T(8,128)(2,1)}, u32[]{:S(2)}, u32[]{:S(2)}) %collective-permute-start.2) | collective-permute-done | bytes 737312 | tf_op jit(solution)/shard_map/ppermute | solution.py:187
  90.0 0.0 all-to-all-done.1.w_ref
  90.0 0.0 all-gather.5.cloned.1.call-update
  90.0 0.1 shard_map.65.w0
  90.1 0.3 collective-permute-start.6
  90.4 2.6 %collective-permute-done.6.w1 = bf16[576,864]{1,0:T(8,128)(2,1)S(1)} collective-permute-done((bf16[576,864]{1,0:T(8,128)(2,1)S(1)}, bf16[576,864]{1,0:T(8,128)(2,1)S(1)}, u32[]{:S(2)}, u32[]{:S(2)}) %collective-permute-start.6) | collective-permute-done | bytes 995360 | tf_op jit(solution)/shard_map/ppermute | solution.py:191
  93.0 17.0 %shard_map.66 = bf16[16,80,288]{2,1,0:T(8,128)(2,1)} custom-call(bf16[320,1152]{1,0:T(8,128)(2,1)S(1)} %bitcast.42, bf16[320,1152]{1,0:T(8,128)(2,1)} %collective-permute-done.2.b, bf16[320,1152]{1,0:T(8,128)(2,1)} %collective-permute-done.3.c_, bf16[320,1152]{1,0:T(8,128)(2,1)} %collective-permute-done.4.d_, bf16[576,864]{1,0:T(8,128)(2,1)S(1)} %shard_map.65.w0, ...), custom_call_target="tpu_custom_call" | custom-call | flops 15000000512 | bytes 15000000 | tf_op jit(solution)/shard_map/pallas_call | solution.py:258
  110.0 0.1 collective-permute-start.8
  110.1 5.3 %all-to-all-start.2 = ((bf16[16,80,288]{2,1,0:T(8,128)(2,1)}), bf16[16,80,288]{2,1,0:T(8,128)(2,1)S(1)}, u32[]{:S(2)}, u32[]{:S(2)}) async-start(bf16[16,80,288]{2,1,0:T(8,128)(2,1)} %shard_map.66), calls=%async_computation.2 | async-start | bytes 1966080 | tf_op jit(solution)/shard_map/all_to_all | solution.py:276
  115.4 3.1 %fusion.5 = (bf16[8,1,72,1152]{3,2,1,0:T(8,128)(2,1)S(1)}, bf16[8,1,72,1152]{3,2,1,0:T(8,128)(2,1)}) fusion(bf16[8,2,72,1152]{3,2,1,0:T(8,128)(2,1)} %bitcast.43), kind=kLoop, calls=%fused_computation.23 | loop fusion | bytes 5308416 | tf_op jit(solution)/shard_map/slice | solution.py:275
  118.4 0.0 collective-permute-done.8
  118.4 3.5 %fusion.4 = (bf16[8,1,72,1152]{3,2,1,0:T(8,128)(2,1)}, bf16[8,1,72,1152]{3,2,1,0:T(8,128)(2,1)}) fusion(bf16[8,2,72,1152]{3,2,1,0:T(8,128)(2,1)} %bitcast.10), kind=kLoop, calls=%fused_computation.22 | loop fusion | bytes 5308416 | tf_op jit(solution)/shard_map/slice | solution.py:275
  121.9 10.7 %all-to-all-done.2.o_ref = bf16[16,80,288]{2,1,0:T(8,128)(2,1)S(1)} async-done(((bf16[16,80,288]{2,1,0:T(8,128)(2,1)}), bf16[16,80,288]{2,1,0:T(8,128)(2,1)S(1)}, u32[]{:S(2)}, u32[]{:S(2)}) %all-to-all-start.2) | async-done | bytes 737312 | tf_op jit(solution)/shard_map/all_to_all | solution.py:276
  132.7 1.3 copy-done.3
  134.0 1.3 copy-done.4
  135.3 0.8 copy-done.6
  136.1 2.8 %shard_map.67 = (f32[320,1152]{1,0:T(8,128)S(1)}, bf16[16,20,1152]{2,1,0:T(8,128)(2,1)S(1)}) custom-call(bf16[16,80,288]{2,1,0:T(8,128)(2,1)S(1)} %all-to-all-done.2.o_ref, bf16[320,1152]{1,0:T(8,128)(2,1)S(1)} %bitcast.34, f32[6,1152]{1,0:T(8,128)S(1)} %copy-done.6, bf16[576,1152]{1,0:T(8,128)(2,1)S(1)} %bitcast.37, bf16[576,1152]{1,0:T(8,128)(2,1)S(1)} %bitcast.38), custom_call_target="tpu_custom_call" | custom-call | flops 4000000000 | bytes 4000000 | tf_op jit(solution)/shard_map/pallas_call | solution.py:278
  138.9 0.9 copy-done.5
  139.9 1.1 copy-done.9
  141.0 5.3 %all-gather.5.cloned.1.call-done.mine_ref = bf16[1920,1152]{1,0:T(8,128)(2,1)} async-done(((bf16[240,1152]{1,0:T(8,128)(2,1)}), bf16[1920,1152]{1,0:T(8,128)(2,1)}) %all-gather.5.cloned.1.call-update) | async-done | bytes 4423696 | tf_op jit(solution)/shard_map/all_gather | solution.py:211
  146.3 0.0 collective-permute-start.9
  146.3 31.5 %all_to_all.25.x_ref = bf16[16,20,1152]{2,1,0:T(8,128)(2,1)S(1)} all-to-all(bf16[16,20,1152]{2,1,0:T(8,128)(2,1)} %copy-done.5), channel_id=1, replica_groups=mesh['frame'=16,'row'=16] {'frame'}, dimensions={0} | all-to-all | bytes 1474560 | tf_op jit(solution)/shard_map/all_to_all | solution.py:283
  177.7 0.0 collective-permute-done.9.other_ref
  177.7 2.3 copy-done.8
  180.0 10.9 %shard_map.68 = bf16[16,20,1152]{2,1,0:T(8,128)(2,1)S(1)} custom-call(bf16[16,20,1152]{2,1,0:T(8,128)(2,1)S(1)} %all_to_all.25.x_ref, bf16[1920,1152]{1,0:T(8,128)(2,1)S(1)} %copy-done.8, bf16[1920,1152]{1,0:T(8,128)(2,1)S(1)} %collective-permute-done.9.other_ref), custom_call_target="tpu_custom_call" | custom-call | flops 12000000000 | bytes 12000000 | tf_op jit(solution)/shard_map/pallas_call | solution.py:284
  190.9 0.0 copy-start.7
  190.9 28.1 %all_to_all.26.o_ref = bf16[16,20,1152]{2,1,0:T(8,128)(2,1)S(1)} all-to-all(bf16[16,20,1152]{2,1,0:T(8,128)(2,1)S(1)} %shard_map.68), channel_id=1, replica_groups=mesh['frame'=16,'row'=16] {'frame'}, dimensions={0} | all-to-all | bytes 1474560 | tf_op jit(solution)/shard_map/all_to_all | solution.py:287
  219.0 2.9 %shard_map.69 = bf16[320,1152]{1,0:T(8,128)(2,1)} custom-call(bf16[16,20,1152]{2,1,0:T(8,128)(2,1)S(1)} %all_to_all.26.o_ref, f32[320,1152]{1,0:T(8,128)S(1)} %copy-done.10, f32[6,1152]{1,0:T(8,128)S(1)} %copy-done.7, bf16[576,1152]{1,0:T(8,128)(2,1)S(1)} %bitcast.35, bf16[576,1152]{1,0:T(8,128)(2,1)S(1)} %bitcast.36), custom_call_target="tpu_custom_call" | custom-call | flops 4000000000 | bytes 4000000 | tf_op jit(solution)/shard_map/pallas_call | solution.py:288
  (27 shorter events, 0.2 us)
Async XLA Ops:
  6.5 3.9 %copy-start = (bf16[1152,216]{0,1:T(8,128)(2,1)S(1)}, bf16[1152,216]{0,1:T(8,128)(2,1)}, u32[]{:S(2)}) copy-start(bf16[1152,216]{0,1:T(8,128)(2,1)} %param.8) | copy-start | bytes 1492996
  6.5 4.1 %copy-start.1 = (bf16[4,2,40,1152]{3,2,1,0:T(8,128)(2,1)S(1)}, bf16[4,2,40,1152]{3,2,1,0:T(8,128)(2,1)}, u32[]{:S(2)}) copy-start(bf16[4,2,40,1152]{3,2,1,0:T(8,128)(2,1)} %param.6) | copy-start | bytes 2211844
  6.5 103.4 %all-gather.3.cloned.1.call-start = ((), (), s32[]{:S(2)}) async-start(), calls=%async_computation.5 | async-start | bytes 2985984 | tf_op jit(solution)/shard_map/all_gather | solution.py:211
  7.9 3.1 %copy-start.11 = (bf16[1152,72]{0,1:T(8,128)(2,1)S(1)}, bf16[1152,72]{0,1:T(8,128)(2,1)}, u32[]{:S(2)}) copy-start(bf16[1152,72]{0,1:T(8,128)(2,1)} %param.11) | copy-start | bytes 497668
  7.9 3.1 %copy-start.12 = (bf16[1152,72]{0,1:T(8,128)(2,1)S(1)}, bf16[1152,72]{0,1:T(8,128)(2,1)}, u32[]{:S(2)}) copy-start(bf16[1152,72]{0,1:T(8,128)(2,1)} %param.9) | copy-start | bytes 497668
  11.1 8.1 %collective-permute-start.7 = (bf16[144,1152]{1,0:T(8,128)(2,1)S(1)}, bf16[144,1152]{1,0:T(8,128)(2,1)S(1)}, u32[]{:S(2)}, u32[]{:S(2)}) collective-permute-start(bf16[144,1152]{1,0:T(8,128)(2,1)S(1)} %pad_maximum_fusion.2), channel_id=1, source_target_pairs={{129,1},{131,3},{133,5},{135,7},{137,9},{139,11},{141,13},{143,15}... | collective-permute-start | bytes 995336 | tf_op jit(solution)/shard_map/ppermute | solution.py:204
  21.0 21.0 %all-to-all-start = ((bf16[16,36,216]{2,1,0:T(8,128)(2,1)}), bf16[16,36,216]{2,1,0:T(8,128)(2,1)S(1)}, u32[]{:S(2)}, u32[]{:S(2)}) async-start(bf16[16,36,216]{2,1,0:T(8,128)(2,1)} %reshape.63), calls=%async_computation | async-start | bytes 655360 | tf_op jit(solution)/shard_map/all_to_all | solution.py:243
  31.5 16.9 %collective-permute-start = (bf16[2,80,1152]{2,1,0:T(8,128)(2,1)S(1)}, bf16[2,80,1152]{2,1,0:T(8,128)(2,1)}, u32[]{:S(2)}, u32[]{:S(2)}) collective-permute-start(bf16[2,80,1152]{2,1,0:T(8,128)(2,1)S(1)} %constant_dynamic-slice_fusion.3), channel_id=1, source_target_pairs={{0,8},{1,9},{2,10},{3,11},{4,12},{5,13},{6,14},{7,15},{8,0},{9,1},... | collective-permute-start | bytes 1105928 | tf_op jit(solution)/shard_map/ppermute | solution.py:195
  43.2 46.7 %all-to-all-start.1 = ((bf16[16,36,864]{2,1,0:T(8,128)(2,1)}), bf16[16,36,864]{2,1,0:T(8,128)(2,1)S(1)}, u32[]{:S(2)}, u32[]{:S(2)}) async-start(bf16[16,36,864]{2,1,0:T(8,128)(2,1)} %broadcast_in_dim.2), calls=%async_computation.1 | async-start | bytes 2293760 | tf_op jit(solution)/shard_map/all_to_all | solution.py:251
  48.3 98.0 %all-gather.5.cloned.1.call-start = ((), (), s32[]{:S(2)}) async-start(), calls=%async_computation.6 | async-start | bytes 4976640 | tf_op jit(solution)/shard_map/all_gather | solution.py:211
  48.3 1.3 copy-start.13
  49.6 3.6 %collective-permute-start.1 = (bf16[2,80,1152]{2,1,0:T(8,128)(2,1)S(1)}, bf16[2,80,1152]{2,1,0:T(8,128)(2,1)S(1)}, u32[]{:S(2)}, u32[]{:S(2)}) collective-permute-start(bf16[2,80,1152]{2,1,0:T(8,128)(2,1)S(1)} %pad_maximum_fusion.1), channel_id=1, source_target_pairs={{0,1},{1,0},{2,3},{3,2},{4,5},{5,4},{6,7},{7,6},{8,9},{9,8},{10,11... | collective-permute-start | bytes 1105928 | tf_op jit(solution)/shard_map/ppermute | solution.py:191
  49.7 14.2 %collective-permute-start.5 = (bf16[240,1152]{1,0:T(8,128)(2,1)S(1)}, bf16[240,1152]{1,0:T(8,128)(2,1)S(1)}, u32[]{:S(2)}, u32[]{:S(2)}) collective-permute-start(bf16[240,1152]{1,0:T(8,128)(2,1)S(1)} %bitcast.44), channel_id=1, source_target_pairs={{129,1},{131,3},{133,5},{135,7},{137,9},{139,11},{141,13},{143,15}... | collective-permute-start | bytes 1658888 | tf_op jit(solution)/shard_map/ppermute | solution.py:204
  53.2 32.9 %collective-permute-start.4 = (bf16[320,1152]{1,0:T(8,128)(2,1)S(1)}, bf16[320,1152]{1,0:T(8,128)(2,1)}, u32[]{:S(2)}, u32[]{:S(2)}) collective-permute-start(bf16[320,1152]{1,0:T(8,128)(2,1)S(1)} %bitcast.39), channel_id=1, source_target_pairs={{0,6},{1,7},{2,0},{3,1},{4,2},{5,3},{6,4},{7,5},{8,14},{9,15},{10,... | collective-permute-start | bytes 2211848 | tf_op jit(solution)/shard_map/ppermute | solution.py:187
  56.1 30.1 %collective-permute-start.3 = (bf16[320,1152]{1,0:T(8,128)(2,1)S(1)}, bf16[320,1152]{1,0:T(8,128)(2,1)}, u32[]{:S(2)}, u32[]{:S(2)}) collective-permute-start(bf16[320,1152]{1,0:T(8,128)(2,1)S(1)} %bitcast.40), channel_id=1, source_target_pairs={{0,4},{1,5},{2,6},{3,7},{4,0},{5,1},{6,2},{7,3},{8,12},{9,13},{10,... | collective-permute-start | bytes 2211848 | tf_op jit(solution)/shard_map/ppermute | solution.py:187
  56.9 33.1 %collective-permute-start.2 = (bf16[320,1152]{1,0:T(8,128)(2,1)S(1)}, bf16[320,1152]{1,0:T(8,128)(2,1)}, u32[]{:S(2)}, u32[]{:S(2)}) collective-permute-start(bf16[320,1152]{1,0:T(8,128)(2,1)S(1)} %bitcast.41), channel_id=1, source_target_pairs={{0,2},{1,3},{2,4},{3,5},{4,6},{5,7},{6,0},{7,1},{8,10},{9,11},{10,... | collective-permute-start | bytes 2211848 | tf_op jit(solution)/shard_map/ppermute | solution.py:187
  90.1 2.9 %collective-permute-start.6 = (bf16[576,864]{1,0:T(8,128)(2,1)S(1)}, bf16[576,864]{1,0:T(8,128)(2,1)S(1)}, u32[]{:S(2)}, u32[]{:S(2)}) collective-permute-start(bf16[576,864]{1,0:T(8,128)(2,1)S(1)} %shard_map.65.w0), channel_id=1, source_target_pairs={{0,1},{1,0},{2,3},{3,2},{4,5},{5,4},{6,7},{7,6},{8,9},{9,8},{10,11... | collective-permute-start | bytes 2985992 | tf_op jit(solution)/shard_map/ppermute | solution.py:191
  110.0 8.5 %collective-permute-start.8 = (bf16[1152,1152]{1,0:T(8,128)(2,1)}, bf16[1152,1152]{1,0:T(8,128)(2,1)}, u32[]{:S(2)}, u32[]{:S(2)}) collective-permute-start(bf16[1152,1152]{1,0:T(8,128)(2,1)} %all-gather.3.cloned.1.call-done), channel_id=1, source_target_pairs={{0,1},{1,0},{2,3},{3,2},{4,5},{5,4},{6,7},{7,6},{8,9},{9,8},{10,11... | collective-permute-start | bytes 7962632 | tf_op jit(solution)/shard_map/ppermute | solution.py:191
  110.1 22.6 %all-to-all-start.2 = ((bf16[16,80,288]{2,1,0:T(8,128)(2,1)}), bf16[16,80,288]{2,1,0:T(8,128)(2,1)S(1)}, u32[]{:S(2)}, u32[]{:S(2)}) async-start(bf16[16,80,288]{2,1,0:T(8,128)(2,1)} %shard_map.66), calls=%async_computation.2 | async-start | bytes 1966080 | tf_op jit(solution)/shard_map/all_to_all | solution.py:276
  132.7 1.3 copy-start.3
  134.0 1.3 copy-start.4
  135.3 0.8 copy-start.6
  138.9 1.0 copy-start.5
  139.9 1.1 copy-start.9
  146.3 31.5 %collective-permute-start.9 = (bf16[1920,1152]{1,0:T(8,128)(2,1)}, bf16[1920,1152]{1,0:T(8,128)(2,1)S(1)}, u32[]{:S(2)}, u32[]{:S(2)}) collective-permute-start(bf16[1920,1152]{1,0:T(8,128)(2,1)} %all-gather.5.cloned.1.call-done.mine_ref), channel_id=1, source_target_pairs={{0,1},{1,0},{2,3},{3,2},{4,5},{5,4},{6,7},{7,6},{8,9},{9,8},{10,11... | collective-permute-start | bytes 13271048 | tf_op jit(solution)/shard_map/ppermute | solution.py:191
  177.7 2.3 copy-start.8
  180.0 39.0 %copy-start.10 = (f32[320,1152]{1,0:T(8,128)S(1)}, f32[320,1152]{1,0:T(8,128)}, u32[]{:S(2)}) copy-start(f32[320,1152]{1,0:T(8,128)} %copy-done.9) | copy-start | bytes 4423684
  190.8 28.1 %copy-start.2 = (bf16[8,1,72,1152]{3,2,1,0:T(8,128)(2,1)S(1)}, bf16[8,1,72,1152]{3,2,1,0:T(8,128)(2,1)}, u32[]{:S(2)}) copy-start(bf16[8,1,72,1152]{3,2,1,0:T(8,128)(2,1)} %get-tuple-element.43) | copy-start | bytes 3981316
  190.9 28.1 %copy-start.7 = (f32[6,1152]{1,0:T(8,128)S(1)}, f32[6,1152]{1,0:T(8,128)}, u32[]{:S(2)}) copy-start(f32[6,1152]{1,0:T(8,128)} %mod_ref.3) | copy-start | bytes 82948
Sparse Core Ops, SparseCore 0:
  20.1 70.0 all-gather.2
  92.0 54.1 all-gather.4
